TPU v7x, 128 devices: a whole 4x4x4 slice. The times are simulated.
128 devices in a mesh: row: 8 (over x, core), col: 16 (over z, y).
Axes of the slice: x: 4, y: 4, z: 4, core: 2. Of those that a mesh axis runs over, the one named last changes fastest.
Arguments:
- density: bfloat16 [6144, 6144], P('row', 'col'), may hold values from -5 to 5
- strips: bfloat16 [16384, 8, 128], P(('row', 'col')), may hold values from -5 to 5
- dest_device: int32 [16384, 1], P(('row', 'col')), may hold values from 0 to 127; in each aligned block of 128 rows (0 to 127, 128 to 255, ...) at most 2 rows name the same one
- atom_slot: int32 [16384], P(('row', 'col')), may hold values from 0 to 95
- block_slot: int32 [16384], P(('row', 'col')), may hold values from 0 to 2
- patterns: int32 [3, 48, 48], replicated, may hold values 0 or 1
Outputs:
- density_next: float32 [6144, 6144], P('row', 'col')
- response_next: float32 [6144, 6144], P('row', 'col')
Inputs may be any that keep to these rules, and one draw needn't show every extreme that they name: `dest_device`: of the 128 strips of one device, at most 2 name the same owner, and some owner is named that often.
All inputs are finite; a program needn't handle non-finite values.
Results may differ from a plain program's by a relative error of at most 0.0036.
Values may be sent and summed in bfloat16 or wider, within the bound.
A program may use at most 128 MiB of HBM per device.

v0:
```python
import math
import jax
import jax.numpy as jnp
from jax import lax
from jax.sharding import PartitionSpec as P

STEPS = 2
CAPACITY = 2


def tile_kept(patterns, which, row_offset, col_offset, block_rows, block_cols, block_width):
    window = lax.dynamic_slice(patterns[which], (row_offset, col_offset), (block_rows, block_cols))
    global_rows = row_offset + lax.iota(jnp.int32, block_rows)
    global_cols = col_offset + lax.iota(jnp.int32, block_cols)
    diagonal = (global_rows[:, None] == global_cols[None, :]).astype(jnp.int32)
    kept = jnp.maximum(window, diagonal).astype(jnp.float32)
    return jnp.repeat(jnp.repeat(kept, block_width, axis=0), block_width, axis=1)


def products(zeroth, linear):
    col_zero, col_first = (
        lax.all_gather(zeroth, "row", axis=0, tiled=True),
        lax.all_gather(linear, "row", axis=0, tiled=True),
    )
    pieces = (
        lax.all_gather(zeroth, "col", axis=1, tiled=True),
        lax.all_gather(linear, "col", axis=1, tiled=True),
    )
    square = jnp.dot(pieces[0], col_zero, preferred_element_type=jnp.float32)
    left_part = jnp.dot(pieces[0], col_first, preferred_element_type=jnp.float32)
    right_part = jnp.dot(pieces[1], col_zero, preferred_element_type=jnp.float32)
    return (square, left_part + right_part)


def on_device(density, strips, dest_device, atom_slot, block_slot, patterns):
    tile_rows, tile_cols = density.shape
    mesh_rows = lax.axis_size("row")
    mesh_cols = lax.axis_size("col")
    devices = mesh_rows * mesh_cols
    matrix_order = tile_rows * mesh_rows
    atom_width = strips.shape[1]
    block_width = strips.shape[2]
    block_rows = tile_rows // block_width
    block_cols = tile_cols // block_width
    row_offset = lax.axis_index("row") * block_rows
    col_offset = lax.axis_index("col") * block_cols
    kept_zero = tile_kept(patterns, 0, row_offset, col_offset, block_rows, block_cols, block_width)
    kept_first = tile_kept(patterns, 1, row_offset, col_offset, block_rows, block_cols, block_width)
    kept_field = tile_kept(patterns, 2, row_offset, col_offset, block_rows, block_cols, block_width)
    capacity = CAPACITY
    targets = dest_device[:, 0]
    matches = (targets[:, None] == lax.iota(jnp.int32, devices)[None, :]).astype(jnp.int32)
    before = jnp.cumsum(matches, axis=0) - matches
    ranking = jnp.sum(before * matches, axis=1)
    position = targets * capacity + ranking
    sent_strips = (
        jnp.zeros((devices * capacity, atom_width, block_width), strips.dtype)
        .at[position]
        .set(strips)
    )
    sent_atoms = jnp.full((devices * capacity,), -1, jnp.int32).at[position].set(atom_slot)
    sent_blocks = jnp.zeros((devices * capacity,), jnp.int32).at[position].set(block_slot)
    arrived = (
        lax.all_to_all(
            sent_strips.reshape(devices, capacity, atom_width, block_width),
            ("row", "col"),
            split_axis=0,
            concat_axis=0,
            tiled=True,
        ),
        lax.all_to_all(
            sent_atoms.reshape(devices, capacity),
            ("row", "col"),
            split_axis=0,
            concat_axis=0,
            tiled=True,
        ),
        lax.all_to_all(
            sent_blocks.reshape(devices, capacity),
            ("row", "col"),
            split_axis=0,
            concat_axis=0,
            tiled=True,
        ),
    )
    recv_strips = arrived[0].reshape(-1, atom_width * block_width)
    recv_atoms = arrived[1].reshape(-1)
    recv_blocks = arrived[2].reshape(-1)
    atoms_here = tile_rows // atom_width
    atom_match = recv_atoms[:, None] == lax.iota(jnp.int32, atoms_here)[None, :]
    block_match = recv_blocks[:, None] == lax.iota(jnp.int32, block_cols)[None, :]
    placing = (
        (atom_match[:, :, None] & block_match[:, None, :])
        .astype(jnp.bfloat16)
        .reshape(-1, atoms_here * block_cols)
    )
    summed = lax.dot_general(
        placing, recv_strips, (((0,), (0,)), ((), ())), preferred_element_type=jnp.float32
    )
    h_field = (
        summed.reshape(atoms_here, block_cols, atom_width, block_width)
        .transpose(0, 2, 1, 3)
        .reshape(tile_rows, tile_cols)
    )
    linear = (-(kept_field * h_field)).astype(jnp.bfloat16)
    zeroth = density
    inv_root = 1.0 / math.sqrt(matrix_order)
    new_zeroth = None
    new_linear = None
    for iteration in range(STEPS):
        square, crossed = products(zeroth, linear)
        if iteration % 2 == 0:
            new_zeroth = kept_zero * (square * inv_root)
            new_linear = kept_first * (crossed * inv_root)
        else:
            new_zeroth = kept_zero * (2.0 * zeroth.astype(jnp.float32) - square * inv_root)
            new_linear = kept_first * (2.0 * linear.astype(jnp.float32) - crossed * inv_root)
        zeroth = new_zeroth.astype(jnp.bfloat16)
        linear = new_linear.astype(jnp.bfloat16)
    return (new_zeroth, new_linear)


def solution(mesh):
    return jax.shard_map(
        on_device,
        mesh=mesh,
        in_specs=(
            P("row", "col"),
            P(("row", "col"), None, None),
            P(("row", "col"), None),
            P(("row", "col")),
            P(("row", "col")),
            P(),
        ),
        out_specs=(P("row", "col"), P("row", "col")),
        check_vma=False,
    )
```

profile of v0, /device:TPU:0, one launch (start us, length us, event | category | flops | bytes accessed | tf_op | source)
XLA Modules:
  0.0 541.6 jit_solution(12071236785653305353)
XLA Ops:
  7.2 0.7 all-gather.11.cloned.1.call-update
  7.9 0.7 fusion.14
  8.7 0.2 reduce_window_sum.11
  8.8 0.8 select_reduce_fusion
  9.7 0.7 fusion.18
  10.3 1.1 scatter_custom_fusion.1
  11.4 0.8 all_to_all.17
  12.2 11.1 %all-to-all-start.1 = ((s32[128,1,2]{2,1,0:T(1,128)}), s32[128,1,2]{2,1,0:T(1,128)S(1)}, u32[]{:S(2)}, u32[]{:S(2)}) async-start(s32[128,1,2]{2,1,0:T(1,128)} %bitcast.10), calls=%async_computation.1 | async-start | bytes 131072 | tf_op jit(solution)/shard_map/all_to_all | solution.py:78
  23.4 0.8 fusion.23
  24.1 0.1 constant_dynamic-slice_fusion
  24.2 0.1 copy.30
  24.3 0.1 copy.31
  24.4 0.1 constant_dynamic-slice_fusion.2
  24.5 0.1 copy.27
  24.6 0.1 fusion.17
  24.7 1.1 scatter_custom_fusion
  25.8 0.8 all_to_all.15
  26.6 6.2 %all-to-all-done.1 = s32[128,1,2]{2,1,0:T(1,128)S(1)} async-done(((s32[128,1,2]{2,1,0:T(1,128)}), s32[128,1,2]{2,1,0:T(1,128)S(1)}, u32[]{:S(2)}, u32[]{:S(2)}) %all-to-all-start.1) | async-done | bytes 1056 | tf_op jit(solution)/shard_map/all_to_all | solution.py:78
  32.8 4.6 all-to-all-start
  37.4 0.1 broadcast_bitcast_fusion
  37.5 0.9 broadcast_in_dim.49
  38.3 13.3 %scatter_fusion = bf16[256,8,128]{2,1,0:T(8,128)(2,1)} fusion(bf16[256,8,128]{2,1,0:T(8,128)(2,1)} %broadcast_in_dim.49, s32[128]{0:T(128)S(1)} %fusion.18, bf16[128,8,128]{2,1,0:T(8,128)(2,1)S(1)} %copy-done.2), kind=kCustom, calls=%fused_computation.2 | custom fusion | bytes 786944 | tf_op jit(solution)/shard_map/scatter | solution.py:59
  51.6 0.6 broadcast.69
  52.2 0.8 reduce.6
  53.1 0.1 eq.91
  53.2 9.8 %all-to-all-start.2 = ((bf16[128,2,8,128]{3,2,1,0:T(8,128)(2,1)}), bf16[128,2,8,128]{3,2,1,0:T(8,128)(2,1)S(1)}, u32[]{:S(2)}, u32[]{:S(2)}) async-start(bf16[128,2,8,128]{3,2,1,0:T(8,128)(2,1)} %bitcast.13), calls=%async_computation.2 | async-start | bytes 1048576 | tf_op jit(solution)/shard_map/all_to_all | solution.py:64
  63.0 0.0 all-gather.19.cloned.1.call-start
  63.1 0.8 reduce.7
  63.9 0.1 eq.87
  64.1 0.1 broadcast_and_fusion
  64.2 0.1 and.22
  64.4 0.1 dot_general.34
  64.5 12.2 %all-to-all-done.2 = bf16[128,2,8,128]{3,2,1,0:T(8,128)(2,1)S(1)} async-done(((bf16[128,2,8,128]{3,2,1,0:T(8,128)(2,1)}), bf16[128,2,8,128]{3,2,1,0:T(8,128)(2,1)S(1)}, u32[]{:S(2)}, u32[]{:S(2)}) %all-to-all-start.2) | async-done | bytes 524320 | tf_op jit(solution)/shard_map/all_to_all | solution.py:64
  76.6 0.1 copy.57
  76.7 0.2 copy.34
  76.9 0.4 convolution_bitcast_fusion.1
  77.3 0.7 copy.56
  78.0 0.4 copy.37
  78.4 0.9 fusion.12
  79.3 0.7 all-gather.17.cloned.1.call-update
  80.1 0.5 all-gather.9.cloned.1.call-update
  80.7 0.1 broadcast_bitcast_fusion.1
  80.7 0.1 broadcast_in_dim.21
  80.8 0.4 copy.40
  81.2 69.7 %all-gather.19.cloned.1.call-done = bf16[768,6144]{0,1:T(8,128)(2,1)} async-done(((bf16[768,384]{0,1:T(8,128)(2,1)}), bf16[768,6144]{0,1:T(8,128)(2,1)}) %all-gather.19.cloned.1.call-update) | async-done | bytes 9437200 | tf_op jit(solution)/shard_map/all_gather | solution.py:27
  150.9 9.0 %fusion.24 = f32[768,384]{1,0:T(8,128)S(1)} fusion(bf16[768,6144]{0,1:T(8,128)(2,1)} %all-gather.19.cloned.1.call-done, bf16[6144,384]{1,0:T(8,128)(2,1)} %all-gather.11.cloned.1.call-done), kind=kOutput, calls=%fused_computation.56 | convolution fusion | flops 3623878656 | bytes 15335424 | tf_op jit(solution)/shard_map/dot_general | solution.py:31
  159.9 27.1 %all-gather.17.cloned.1.call-done = bf16[6144,384]{0,1:T(8,128)(2,1)} async-done(((bf16[768,384]{0,1:T(8,128)(2,1)}), bf16[6144,384]{0,1:T(8,128)(2,1)}) %all-gather.17.cloned.1.call-update) | async-done | bytes 4718608 | tf_op jit(solution)/shard_map/all_gather | solution.py:23
  187.1 85.9 %all-gather.9.cloned.1.call-done = bf16[768,6144]{1,0:T(8,128)(2,1)} async-done(((bf16[768,384]{1,0:T(8,128)(2,1)}), bf16[768,6144]{1,0:T(8,128)(2,1)}) %all-gather.9.cloned.1.call-update) | async-done | bytes 9437200 | tf_op jit(solution)/shard_map/all_gather | solution.py:26
  272.9 9.8 %fusion.9 = bf16[768,384]{1,0:T(8,128)(2,1)} fusion(f32[768,384]{1,0:T(8,128)S(1)} %copy.40, f32[768,384]{1,0:T(8,128)S(1)} %fusion.24, bf16[6144,384]{0,1:T(8,128)(2,1)} %all-gather.17.cloned.1.call-done, bf16[768,6144]{1,0:T(8,128)(2,1)} %all-gather.9.cloned.1.call-done), kind=kOutput, calls=%fused_computation.17 | convolution fusion | flops 3625058304 | bytes 17104896 | tf_op jit(solution)/shard_map/dot_general | solution.py:30
  282.8 0.2 all-gather.13.cloned.1.call-start
  283.0 0.1 broadcast_bitcast_fusion.2
  283.1 0.1 broadcast_in_dim.19
  283.2 0.4 copy.29
  283.5 9.7 %fusion.10 = bf16[768,384]{1,0:T(8,128)(2,1)} fusion(f32[768,384]{1,0:T(8,128)S(1)} %copy.29, bf16[768,6144]{1,0:T(8,128)(2,1)} %all-gather.9.cloned.1.call-done, bf16[6144,384]{1,0:T(8,128)(2,1)} %all-gather.11.cloned.1.call-done), kind=kOutput, calls=%fused_computation.18 | convolution fusion | flops 3624763392 | bytes 15925248 | tf_op jit(solution)/shard_map/dot_general | solution.py:29
  293.3 0.0 all-gather.15.cloned.1.call-start
  293.3 0.7 all-gather.15.cloned.1.call-update
  294.1 0.7 all-gather.23.cloned.1.call-update
  294.8 21.6 %all-gather.21.cloned.1.call-done = bf16[6144,384]{1,0:T(8,128)(2,1)} async-done(((bf16[768,384]{1,0:T(8,128)(2,1)}), bf16[6144,384]{1,0:T(8,128)(2,1)}) %all-gather.21.cloned.1.call-update) | async-done | bytes 4718608 | tf_op jit(solution)/shard_map/all_gather | solution.py:23
  316.4 86.4 %all-gather.13.cloned.1.call-done = bf16[768,6144]{1,0:T(8,128)(2,1)} async-done(((bf16[768,384]{1,0:T(8,128)(2,1)}), bf16[768,6144]{1,0:T(8,128)(2,1)}) %all-gather.13.cloned.1.call-update) | async-done | bytes 9437200 | tf_op jit(solution)/shard_map/all_gather | solution.py:26
  402.9 9.8 %fusion.25 = f32[768,384]{1,0:T(8,128)} fusion(bf16[768,6144]{1,0:T(8,128)(2,1)} %all-gather.13.cloned.1.call-done, bf16[6144,384]{1,0:T(8,128)(2,1)} %all-gather.21.cloned.1.call-done), kind=kOutput, calls=%fused_computation.57 | convolution fusion | flops 3623878656 | bytes 15335424 | tf_op jit(solution)/shard_map/dot_general | solution.py:30
  412.6 26.0 %all-gather.15.cloned.1.call-done = bf16[6144,384]{1,0:T(8,128)(2,1)} async-done(((bf16[768,384]{1,0:T(8,128)(2,1)}), bf16[6144,384]{1,0:T(8,128)(2,1)}) %all-gather.15.cloned.1.call-update) | async-done | bytes 4718608 | tf_op jit(solution)/shard_map/all_gather | solution.py:22
  438.7 9.8 %fusion.2 = f32[768,384]{1,0:T(8,128)} fusion(f32[768,384]{1,0:T(8,128)S(1)} %copy.29, bf16[768,6144]{1,0:T(8,128)(2,1)} %all-gather.13.cloned.1.call-done, bf16[6144,384]{1,0:T(8,128)(2,1)} %all-gather.15.cloned.1.call-done, bf16[768,384]{1,0:T(8,128)(2,1)S(1)} %copy-done.1), kind=kOutput, calls=%fused_computation.9 | convolution fusion | flops 3625353216 | bytes 17104896 | tf_op jit(solution)/shard_map/dot_general | solution.py:29
  448.5 76.2 %all-gather.23.cloned.1.call-done = bf16[768,6144]{1,0:T(8,128)(2,1)} async-done(((bf16[768,384]{1,0:T(8,128)(2,1)}), bf16[768,6144]{1,0:T(8,128)(2,1)}) %all-gather.23.cloned.1.call-update) | async-done | bytes 9437200 | tf_op jit(solution)/shard_map/all_gather | solution.py:27
  524.7 10.1 %fusion.8 = f32[768,384]{1,0:T(8,128)} fusion(f32[768,384]{1,0:T(8,128)S(1)} %copy.40, f32[768,384]{1,0:T(8,128)} %fusion.25, bf16[768,6144]{1,0:T(8,128)(2,1)} %all-gather.23.cloned.1.call-done, bf16[6144,384]{1,0:T(8,128)(2,1)} %all-gather.15.cloned.1.call-done, bf16[768,384]{1,0:T(8,128)(2,1)S(1)} %copy-done), kind=kOutput, calls=%fused_computation.16 | convolution fusion | flops 3625648128 | bytes 18284544 | tf_op jit(solution)/shard_map/dot_general | solution.py:31
  (23 shorter events, 0.3 us)
Async XLA Ops:
  7.2 31.2 %copy-start.2 = (bf16[128,8,128]{2,1,0:T(8,128)(2,1)S(1)}, bf16[128,8,128]{2,1,0:T(8,128)(2,1)}, u32[]{:S(2)}) copy-start(bf16[128,8,128]{2,1,0:T(8,128)(2,1)} %param.7) | copy-start | bytes 786436
  7.2 74.1 %all-gather.11.cloned.1.call-start = ((), (), s32[]{:S(2)}) async-start(), calls=%async_computation.4 | async-start | bytes 5308416 | tf_op jit(solution)/shard_map/all_gather | solution.py:22
  12.2 20.6 %all-to-all-start.1 = ((s32[128,1,2]{2,1,0:T(1,128)}), s32[128,1,2]{2,1,0:T(1,128)S(1)}, u32[]{:S(2)}, u32[]{:S(2)}) async-start(s32[128,1,2]{2,1,0:T(1,128)} %bitcast.10), calls=%async_computation.1 | async-start | bytes 131072 | tf_op jit(solution)/shard_map/all_to_all | solution.py:78
  32.8 20.5 %all-to-all-start = ((s32[128,1,2]{2,1,0:T(1,128)}), s32[128,1,2]{2,1,0:T(1,128)S(1)}, u32[]{:S(2)}, u32[]{:S(2)}) async-start(s32[128,1,2]{2,1,0:T(1,128)} %bitcast.9), calls=%async_computation | async-start | bytes 131072 | tf_op jit(solution)/shard_map/all_to_all | solution.py:71
  53.2 23.4 %all-to-all-start.2 = ((bf16[128,2,8,128]{3,2,1,0:T(8,128)(2,1)}), bf16[128,2,8,128]{3,2,1,0:T(8,128)(2,1)S(1)}, u32[]{:S(2)}, u32[]{:S(2)}) async-start(bf16[128,2,8,128]{3,2,1,0:T(8,128)(2,1)} %bitcast.13), calls=%async_computation.2 | async-start | bytes 1048576 | tf_op jit(solution)/shard_map/all_to_all | solution.py:64
  63.0 87.9 %all-gather.19.cloned.1.call-start = ((), (), s32[]{:S(2)}) async-start(), calls=%async_computation.8 | async-start | bytes 10027008 | tf_op jit(solution)/shard_map/all_gather | solution.py:27
  79.3 107.8 %all-gather.17.cloned.1.call-start = ((), (), s32[]{:S(2)}) async-start(), calls=%async_computation.7 | async-start | bytes 5308416 | tf_op jit(solution)/shard_map/all_gather | solution.py:23
  80.0 192.9 %all-gather.9.cloned.1.call-start = ((), (), s32[]{:S(2)}) async-start(), calls=%async_computation.3 | async-start | bytes 10027008 | tf_op jit(solution)/shard_map/all_gather | solution.py:26
  80.6 235.8 %all-gather.21.cloned.1.call-start = ((), (), s32[]{:S(2)}) async-start(), calls=%async_computation.9 | async-start | bytes 5308416 | tf_op jit(solution)/shard_map/all_gather | solution.py:23
  282.8 120.1 %all-gather.13.cloned.1.call-start = ((), (), s32[]{:S(2)}) async-start(), calls=%async_computation.5 | async-start | bytes 10027008 | tf_op jit(solution)/shard_map/all_gather | solution.py:26
  293.3 145.4 %all-gather.15.cloned.1.call-start = ((), (), s32[]{:S(2)}) async-start(), calls=%async_computation.6 | async-start | bytes 5308416 | tf_op jit(solution)/shard_map/all_gather | solution.py:22
  294.0 230.6 %all-gather.23.cloned.1.call-start = ((), (), s32[]{:S(2)}) async-start(), calls=%async_computation.10 | async-start | bytes 10027008 | tf_op jit(solution)/shard_map/all_gather | solution.py:27
  294.8 143.9 %copy-start.1 = (bf16[768,384]{1,0:T(8,128)(2,1)S(1)}, bf16[768,384]{1,0:T(8,128)(2,1)}, u32[]{:S(2)}) copy-start(bf16[768,384]{1,0:T(8,128)(2,1)} %fusion.10) | copy-start | bytes 1769476
  412.6 112.0 %copy-start = (bf16[768,384]{1,0:T(8,128)(2,1)S(1)}, bf16[768,384]{1,0:T(8,128)(2,1)}, u32[]{:S(2)}) copy-start(bf16[768,384]{1,0:T(8,128)(2,1)} %fusion.9) | copy-start | bytes 1769476
Sparse Core Ops, SparseCore 0:
  9.7 38.0 all-gather.10
  79.4 71.4 all-gather.18
  153.2 33.8 all-gather.16
  189.0 83.8 all-gather.8
  282.9 33.4 all-gather.20
  319.0 83.8 all-gather.12
  405.1 33.4 all-gather.14
  440.8 83.8 all-gather.22
where the time goes:
time: 542 us
  waiting for transfers between devices  415 us (77%)
  matrix products  58.5 us (11%)
  starting transfers between devices  26 us (5%)
  local copies, waits for them, and re-layouts  22.7 us (4%)
  between operations  14.4 us (3%)
    all_gather x2, waiting for transfers between devices, products(): lax.all_gather(zeroth, 'col', axis=1, tiled=True)  172 us
    all_gather x2, waiting for transfers between devices, products(): lax.all_gather(linear, 'col', axis=1, tiled=True)  146 us
    all_gather x2, waiting for transfers between devices, products(): lax.all_gather(linear, 'row', axis=0, tiled=True)  48.8 us
    all_gather x2, waiting for transfers between devices, products(): lax.all_gather(zeroth, 'row', axis=0, tiled=True)  26 us
    dot_general x2, matrix products, products(): jnp.dot(pieces[0], col_first, preferred_element_type=jnp.float32)  19.6 us
    dot_general x2, matrix products, products(): square = jnp.dot(pieces[0], col_zero, preferred_element_type=jnp.float32)  19.5 us
    dot_general x2, matrix products, products(): jnp.dot(pieces[1], col_zero, preferred_element_type=jnp.float32)  19.1 us
    scatter x1, local copies, waits for them, and re-layouts, on_device(): sent_strips = jnp.zeros((devices * capacity, atom_width, block_width), st...  13.3 us
  transfers between devices with their start and end apart: 11, of which 9 were waited for; matrix products, arithmetic and copies ran while one was open for 12% of the time, Pallas kernels for 0%

commit v1 on v0

--- a/solution.py
+++ b/solution.py
@@ -19,7 +19,9 @@
 
 def products(zeroth, linear):
     col_zero, col_first = (
-        lax.all_gather(zeroth, "row", axis=0, tiled=True),
+        jnp.concatenate(
+            lax.all_to_all(jnp.stack([zeroth] * lax.axis_size("row")), "row", 0, 0), axis=0
+        ),
         lax.all_gather(linear, "row", axis=0, tiled=True),
     )
     pieces = (

time: 542 us -> 522 us (0.963)
  waiting for transfers between devices: 415 us -> 379 us
  starting transfers between devices: 26 us -> 35.4 us
    all_gather x2, waiting for transfers between devices: 146 us -> 72.6 us  [products(): lax.all_gather(linear, 'col', axis=1, tiled=True)]
    all_to_all x0 -> x2, waiting for transfers between devices: none -> 54.5 us  [products(): lax.all_to_all(jnp.stack([zeroth] * lax.axis_size('row')), 'row', 0, 0)]
    all_gather x2 -> x0, waiting for transfers between devices: 26 us -> none  [products(): lax.all_gather(zeroth, 'row', axis=0, tiled=True)]
    all_to_all x0 -> x2, starting transfers between devices: none -> 9.46 us  [products(): lax.all_to_all(jnp.stack([zeroth] * lax.axis_size('row')), 'row', 0, 0)]
    all_gather x2, waiting for transfers between devices: 48.8 us -> 57.6 us  [products(): lax.all_gather(linear, 'row', axis=0, tiled=True)]
where the time goes in v1:
time: 522 us; the launch traced here: 521 us
  waiting for transfers between devices  379 us (73%)
  matrix products  59.1 us (11%)
  starting transfers between devices  35.4 us (7%)
  local copies, waits for them, and re-layouts  28.1 us (5%)
  between operations  14.4 us (3%)
    all_gather x2, waiting for transfers between devices, products(): lax.all_gather(zeroth, 'col', axis=1, tiled=True)  174 us
    all_gather x2, waiting for transfers between devices, products(): lax.all_gather(linear, 'col', axis=1, tiled=True)  72.6 us
    all_gather x2, waiting for transfers between devices, products(): lax.all_gather(linear, 'row', axis=0, tiled=True)  57.6 us
    all_to_all x2, waiting for transfers between devices, products(): lax.all_to_all(jnp.stack([zeroth] * lax.axis_size('row')), 'row', 0, 0)  54.5 us
    dot_general x2, matrix products, products(): square = jnp.dot(pieces[0], col_zero, preferred_element_type=jnp.float32)  20.1 us
    dot_general x2, matrix products, products(): jnp.dot(pieces[0], col_first, preferred_element_type=jnp.float32)  19.6 us
    dot_general x2, matrix products, products(): jnp.dot(pieces[1], col_zero, preferred_element_type=jnp.float32)  19.1 us
    scatter x1, local copies, waits for them, and re-layouts, on_device(): sent_strips = jnp.zeros((devices * capacity, atom_width, block_width), st...  13.3 us
  transfers between devices with their start and end apart: 11, of which 9 were waited for; matrix products, arithmetic and copies ran while one was open for 12% of the time, Pallas kernels for 0%

profile of v1, /device:TPU:0, one launch (start us, length us, event | category | flops | bytes accessed | tf_op | source)
XLA Modules:
  0.0 521.2 jit_solution(15566777242646159375)
XLA Ops:
  7.2 0.8 fusion.14
  8.0 0.2 reduce_window_sum.11
  8.1 0.8 select_reduce_fusion
  9.0 0.7 fusion.18
  9.6 1.1 scatter_custom_fusion.1
  10.7 0.8 all_to_all.25
  11.5 11.1 %all-to-all-start.3 = ((s32[128,1,2]{2,1,0:T(1,128)}), s32[128,1,2]{2,1,0:T(1,128)S(1)}, u32[]{:S(2)}, u32[]{:S(2)}) async-start(s32[128,1,2]{2,1,0:T(1,128)} %bitcast.12), calls=%async_computation.3 | async-start | bytes 131072 | tf_op jit(solution)/shard_map/all_to_all | solution.py:80
  22.7 0.8 fusion.23
  23.5 0.1 constant_dynamic-slice_fusion
  23.6 0.1 copy.30
  23.7 0.1 copy.31
  23.7 0.1 constant_dynamic-slice_fusion.2
  23.8 0.1 copy.27
  23.9 0.1 fusion.17
  24.0 1.1 scatter_custom_fusion
  25.1 0.8 all_to_all.23
  25.9 6.2 %all-to-all-done.3 = s32[128,1,2]{2,1,0:T(1,128)S(1)} async-done(((s32[128,1,2]{2,1,0:T(1,128)}), s32[128,1,2]{2,1,0:T(1,128)S(1)}, u32[]{:S(2)}, u32[]{:S(2)}) %all-to-all-start.3) | async-done | bytes 1056 | tf_op jit(solution)/shard_map/all_to_all | solution.py:80
  32.1 4.6 all-to-all-start.2
  36.7 0.1 broadcast_bitcast_fusion
  36.8 0.9 broadcast_in_dim.49
  37.6 13.3 %scatter_fusion = bf16[256,8,128]{2,1,0:T(8,128)(2,1)} fusion(bf16[256,8,128]{2,1,0:T(8,128)(2,1)} %broadcast_in_dim.49, s32[128]{0:T(128)S(1)} %fusion.18, bf16[128,8,128]{2,1,0:T(8,128)(2,1)S(1)} %copy-done.3), kind=kCustom, calls=%fused_computation.2 | custom fusion | bytes 786944 | tf_op jit(solution)/shard_map/scatter | solution.py:61
  50.9 0.5 broadcast.73
  51.4 0.7 reduce.6
  52.1 0.1 eq.91
  52.3 9.8 %all-to-all-start.4 = ((bf16[128,2,8,128]{3,2,1,0:T(8,128)(2,1)}), bf16[128,2,8,128]{3,2,1,0:T(8,128)(2,1)S(1)}, u32[]{:S(2)}, u32[]{:S(2)}) async-start(bf16[128,2,8,128]{3,2,1,0:T(8,128)(2,1)} %bitcast.15), calls=%async_computation.4 | async-start | bytes 1048576 | tf_op jit(solution)/shard_map/all_to_all | solution.py:66
  62.1 0.7 reduce.7
  62.8 0.1 eq.87
  63.0 0.1 broadcast_and_fusion
  63.1 0.1 and.22
  63.3 0.1 dot_general.34
  63.4 12.3 %all-to-all-done.4 = bf16[128,2,8,128]{3,2,1,0:T(8,128)(2,1)S(1)} async-done(((bf16[128,2,8,128]{3,2,1,0:T(8,128)(2,1)}), bf16[128,2,8,128]{3,2,1,0:T(8,128)(2,1)S(1)}, u32[]{:S(2)}, u32[]{:S(2)}) %all-to-all-start.4) | async-done | bytes 524320 | tf_op jit(solution)/shard_map/all_to_all | solution.py:66
  75.7 0.1 copy.57
  75.8 0.2 copy.34
  76.0 0.4 convolution_bitcast_fusion.1
  76.3 0.7 copy.56
  77.0 0.4 copy.37
  77.4 0.9 fusion.12
  78.4 0.7 all-gather.11.cloned.1.call-update
  79.1 0.7 all-gather.7.cloned.1.call-update
  79.8 2.5 stack.4
  82.4 4.6 all-to-all-start
  87.0 0.2 all-gather.15.cloned.1.call-start
  87.3 0.1 broadcast_in_dim.21
  87.4 0.4 copy.40
  87.8 54.5 %all-to-all-done = bf16[8,768,384]{2,1,0:T(8,128)(2,1)} async-done(((bf16[8,768,384]{2,1,0:T(8,128)(2,1)}), bf16[8,768,384]{2,1,0:T(8,128)(2,1)}, u32[]{:S(2)}, u32[]{:S(2)}) %all-to-all-start) | async-done | bytes 4718624 | tf_op jit(solution)/shard_map/all_to_all | solution.py:23
  142.3 7.7 %all-gather.13.cloned.1.call-done = bf16[768,6144]{0,1:T(8,128)(2,1)} async-done(((bf16[768,384]{0,1:T(8,128)(2,1)}), bf16[768,6144]{0,1:T(8,128)(2,1)}) %all-gather.13.cloned.1.call-update) | async-done | bytes 9437200 | tf_op jit(solution)/shard_map/all_gather | solution.py:29
  150.0 9.0 %fusion.24 = f32[768,384]{1,0:T(8,128)S(1)} fusion(bf16[768,6144]{0,1:T(8,128)(2,1)} %all-gather.13.cloned.1.call-done, bf16[6144,384]{1,0:T(8,128)(2,1)} %bitcast.2), kind=kOutput, calls=%fused_computation.56 | convolution fusion | flops 3623878656 | bytes 15335424 | tf_op jit(solution)/shard_map/dot_general | solution.py:33
  159.0 27.1 %all-gather.11.cloned.1.call-done = bf16[6144,384]{0,1:T(8,128)(2,1)} async-done(((bf16[768,384]{0,1:T(8,128)(2,1)}), bf16[6144,384]{0,1:T(8,128)(2,1)}) %all-gather.11.cloned.1.call-update) | async-done | bytes 4718608 | tf_op jit(solution)/shard_map/all_gather | solution.py:25
  186.1 86.0 %all-gather.7.cloned.1.call-done = bf16[768,6144]{1,0:T(8,128)(2,1)} async-done(((bf16[768,384]{1,0:T(8,128)(2,1)}), bf16[768,6144]{1,0:T(8,128)(2,1)}) %all-gather.7.cloned.1.call-update) | async-done | bytes 9437200 | tf_op jit(solution)/shard_map/all_gather | solution.py:28
  272.1 9.8 %fusion.9 = bf16[768,384]{1,0:T(8,128)(2,1)} fusion(f32[768,384]{1,0:T(8,128)S(1)} %copy.40, f32[768,384]{1,0:T(8,128)S(1)} %fusion.24, bf16[6144,384]{0,1:T(8,128)(2,1)} %all-gather.11.cloned.1.call-done, bf16[768,6144]{1,0:T(8,128)(2,1)} %all-gather.7.cloned.1.call-done), kind=kOutput, calls=%fused_computation.17 | convolution fusion | flops 3625058304 | bytes 17104896 | tf_op jit(solution)/shard_map/dot_general | solution.py:32
  282.0 0.1 broadcast_bitcast_fusion.2
  282.1 0.1 broadcast_in_dim.19
  282.2 0.4 copy.29
  282.5 9.7 %fusion.10 = bf16[768,384]{1,0:T(8,128)(2,1)} fusion(f32[768,384]{1,0:T(8,128)S(1)} %copy.29, bf16[768,6144]{1,0:T(8,128)(2,1)} %all-gather.7.cloned.1.call-done, bf16[6144,384]{1,0:T(8,128)(2,1)} %bitcast.2), kind=kOutput, calls=%fused_computation.18 | convolution fusion | flops 3624763392 | bytes 15925248 | tf_op jit(solution)/shard_map/dot_general | solution.py:31
  292.3 0.5 all-gather.17.cloned.1.call-update
  292.8 0.5 copy-done.2
  293.3 2.5 stack.5
  295.8 4.8 all-to-all-start.1
  300.7 30.5 %all-gather.15.cloned.1.call-done = bf16[6144,384]{1,0:T(8,128)(2,1)} async-done(((bf16[768,384]{1,0:T(8,128)(2,1)}), bf16[6144,384]{1,0:T(8,128)(2,1)}) %all-gather.15.cloned.1.call-update) | async-done | bytes 4718608 | tf_op jit(solution)/shard_map/all_gather | solution.py:25
  331.1 88.1 %all-gather.9.cloned.1.call-done = bf16[768,6144]{1,0:T(8,128)(2,1)} async-done(((bf16[768,384]{1,0:T(8,128)(2,1)}), bf16[768,6144]{1,0:T(8,128)(2,1)}) %all-gather.9.cloned.1.call-update) | async-done | bytes 9437200 | tf_op jit(solution)/shard_map/all_gather | solution.py:28
  419.2 9.8 %fusion.25 = f32[768,384]{1,0:T(8,128)} fusion(bf16[768,6144]{1,0:T(8,128)(2,1)} %all-gather.9.cloned.1.call-done, bf16[6144,384]{1,0:T(8,128)(2,1)} %all-gather.15.cloned.1.call-done), kind=kOutput, calls=%fused_computation.57 | convolution fusion | flops 3623878656 | bytes 15335424 | tf_op jit(solution)/shard_map/dot_general | solution.py:32
  429.0 10.4 %fusion.2 = f32[768,384]{1,0:T(8,128)} fusion(f32[768,384]{1,0:T(8,128)S(1)} %copy.29, bf16[768,6144]{1,0:T(8,128)(2,1)} %all-gather.9.cloned.1.call-done, bf16[6144,384]{1,0:T(8,128)(2,1)} %bitcast.3, bf16[768,384]{1,0:T(8,128)(2,1)S(1)} %copy-done.2), kind=kOutput, calls=%fused_computation.9 | convolution fusion | flops 3625353216 | bytes 17104896 | tf_op jit(solution)/shard_map/dot_general | solution.py:31
  439.4 64.9 %all-gather.17.cloned.1.call-done = bf16[768,6144]{1,0:T(8,128)(2,1)} async-done(((bf16[768,384]{1,0:T(8,128)(2,1)}), bf16[768,6144]{1,0:T(8,128)(2,1)}) %all-gather.17.cloned.1.call-update) | async-done | bytes 9437200 | tf_op jit(solution)/shard_map/all_gather | solution.py:29
  504.3 10.1 %fusion.8 = f32[768,384]{1,0:T(8,128)} fusion(f32[768,384]{1,0:T(8,128)S(1)} %copy.40, f32[768,384]{1,0:T(8,128)} %fusion.25, bf16[768,6144]{1,0:T(8,128)(2,1)} %all-gather.17.cloned.1.call-done, bf16[6144,384]{1,0:T(8,128)(2,1)} %bitcast.3, bf16[768,384]{1,0:T(8,128)(2,1)S(1)} %copy-done), kind=kOutput, calls=%fused_computation.16 | convolution fusion | flops 3625648128 | bytes 18284544 | tf_op jit(solution)/shard_map/dot_general | solution.py:33
  (25 shorter events, 0.4 us)
Async XLA Ops:
  7.2 30.5 %copy-start.3 = (bf16[128,8,128]{2,1,0:T(8,128)(2,1)S(1)}, bf16[128,8,128]{2,1,0:T(8,128)(2,1)}, u32[]{:S(2)}) copy-start(bf16[128,8,128]{2,1,0:T(8,128)(2,1)} %param.7) | copy-start | bytes 786436
  11.5 20.6 %all-to-all-start.3 = ((s32[128,1,2]{2,1,0:T(1,128)}), s32[128,1,2]{2,1,0:T(1,128)S(1)}, u32[]{:S(2)}, u32[]{:S(2)}) async-start(s32[128,1,2]{2,1,0:T(1,128)} %bitcast.12), calls=%async_computation.3 | async-start | bytes 131072 | tf_op jit(solution)/shard_map/all_to_all | solution.py:80
  32.1 20.2 %all-to-all-start.2 = ((s32[128,1,2]{2,1,0:T(1,128)}), s32[128,1,2]{2,1,0:T(1,128)S(1)}, u32[]{:S(2)}, u32[]{:S(2)}) async-start(s32[128,1,2]{2,1,0:T(1,128)} %bitcast.11), calls=%async_computation.2 | async-start | bytes 131072 | tf_op jit(solution)/shard_map/all_to_all | solution.py:73
  52.3 23.4 %all-to-all-start.4 = ((bf16[128,2,8,128]{3,2,1,0:T(8,128)(2,1)}), bf16[128,2,8,128]{3,2,1,0:T(8,128)(2,1)S(1)}, u32[]{:S(2)}, u32[]{:S(2)}) async-start(bf16[128,2,8,128]{3,2,1,0:T(8,128)(2,1)} %bitcast.15), calls=%async_computation.4 | async-start | bytes 1048576 | tf_op jit(solution)/shard_map/all_to_all | solution.py:66
  62.1 87.9 %all-gather.13.cloned.1.call-start = ((), (), s32[]{:S(2)}) async-start(), calls=%async_computation.8 | async-start | bytes 10027008 | tf_op jit(solution)/shard_map/all_gather | solution.py:29
  78.3 1.5 copy-start.1
  78.3 107.8 %all-gather.11.cloned.1.call-start = ((), (), s32[]{:S(2)}) async-start(), calls=%async_computation.7 | async-start | bytes 5308416 | tf_op jit(solution)/shard_map/all_gather | solution.py:25
  79.1 193.0 %all-gather.7.cloned.1.call-start = ((), (), s32[]{:S(2)}) async-start(), calls=%async_computation.5 | async-start | bytes 10027008 | tf_op jit(solution)/shard_map/all_gather | solution.py:28
  82.4 59.9 %all-to-all-start = ((bf16[8,768,384]{2,1,0:T(8,128)(2,1)}), bf16[8,768,384]{2,1,0:T(8,128)(2,1)}, u32[]{:S(2)}, u32[]{:S(2)}) async-start(bf16[8,768,384]{2,1,0:T(8,128)(2,1)} %stack.4), calls=%async_computation | async-start | bytes 9437184 | tf_op jit(solution)/shard_map/all_to_all | solution.py:23
  87.0 244.1 %all-gather.15.cloned.1.call-start = ((), (), s32[]{:S(2)}) async-start(), calls=%async_computation.9 | async-start | bytes 5308416 | tf_op jit(solution)/shard_map/all_gather | solution.py:25
  281.9 137.3 %all-gather.9.cloned.1.call-start = ((), (), s32[]{:S(2)}) async-start(), calls=%async_computation.6 | async-start | bytes 10027008 | tf_op jit(solution)/shard_map/all_gather | solution.py:28
  292.2 1.1 copy-start.2
  292.3 212.0 %all-gather.17.cloned.1.call-start = ((), (), s32[]{:S(2)}) async-start(), calls=%async_computation.10 | async-start | bytes 10027008 | tf_op jit(solution)/shard_map/all_gather | solution.py:29
  295.8 133.2 %all-to-all-start.1 = ((bf16[8,768,384]{2,1,0:T(8,128)(2,1)}), bf16[8,768,384]{2,1,0:T(8,128)(2,1)}, u32[]{:S(2)}, u32[]{:S(2)}) async-start(bf16[8,768,384]{2,1,0:T(8,128)(2,1)} %stack.5), calls=%async_computation.1 | async-start | bytes 9437184 | tf_op jit(solution)/shard_map/all_to_all | solution.py:23
  429.0 75.3 %copy-start = (bf16[768,384]{1,0:T(8,128)(2,1)S(1)}, bf16[768,384]{1,0:T(8,128)(2,1)}, u32[]{:S(2)}) copy-start(bf16[768,384]{1,0:T(8,128)(2,1)} %fusion.9) | copy-start | bytes 1769476
Sparse Core Ops, SparseCore 0:
  78.5 71.4 all-gather.12
  152.2 33.8 all-gather.10
  188.2 83.8 all-gather.6
  282.1 49.0 all-gather.14
  333.7 85.4 all-gather.8
  421.2 83.0 all-gather.16
